TPU v7x, 128 devices: a whole 4x4x4 slice. The times are simulated.
128 devices in a mesh: rep: 2 (over z_hi), fsdp: 64 (over z_lo, x, y, core).
Axes of the slice: x: 4, y: 4, z: 4 (z_hi: 2, z_lo: 2; z = z_hi * 2 + z_lo), core: 2. Of those that a mesh axis runs over, the one named last changes fastest.
Arguments:
- tokens: bfloat16 [32768, 1024], P(('rep', 'fsdp')), may hold values from -6 to 6
- gain_first: bfloat16 [1024], P('fsdp'), may hold values from 0.099609375 to 1.8984375
- w_in: bfloat16 [1024, 3072], P('fsdp'), may hold values from -0.1875 to 0.1875
- conv_weight: bfloat16 [1024, 3], P('fsdp'), may hold values from -3.5 to 3.5
- w_out: bfloat16 [1024, 1024], P('fsdp'), may hold values from -0.1875 to 0.1875
- gain_second: bfloat16 [1024], P('fsdp'), may hold values from 0.099609375 to 1.8984375
- w_gate: bfloat16 [1024, 4608], P('fsdp'), may hold values from -0.1875 to 0.1875
- w_up: bfloat16 [1024, 4608], P('fsdp'), may hold values from -0.1875 to 0.1875
- w_down: bfloat16 [4608, 1024], P('fsdp'), may hold values from -0.09375 to 0.09375
- cotangent: bfloat16 [32768, 1024], P(('rep', 'fsdp')), may hold values from -6 to 6
Outputs:
- result: bfloat16 [32768, 1024], P(('rep', 'fsdp'))
- grad_tokens: float32 [32768, 1024], P(('rep', 'fsdp'))
- grad_gain_first: float32 [1024], P('fsdp')
- grad_w_in: float32 [1024, 3072], P('fsdp')
- grad_conv_weight: float32 [1024, 3], P('fsdp')
- grad_w_out: float32 [1024, 1024], P('fsdp')
- grad_gain_second: float32 [1024], P('fsdp')
- grad_w_gate: float32 [1024, 4608], P('fsdp')
- grad_w_up: float32 [1024, 4608], P('fsdp')
- grad_w_down: float32 [4608, 1024], P('fsdp')
All inputs are finite; a program needn't handle non-finite values.
Results may differ from a plain program's by a relative error of at most 0.012.
Values may be sent and summed in bfloat16 or wider, within the bound.
No kernel may reach another device: no remote copies, remote signals or barrier semaphores. Data moves between devices by JAX's collectives and lax.ppermute only.
A program may use at most 256 MiB of HBM per device.

v0:
```python
import jax
import jax.numpy as jnp
from jax import lax
from jax.sharding import PartitionSpec as P

epsilon = 1e-05


def passed_along(value, axis, steps):
    count = lax.axis_size(axis)
    first, last = (max(0, -steps), min(count, count - steps))
    return lax.ppermute(value, axis, [(source, source + steps) for source in range(first, last)])


def norm_scale(values):
    return lax.rsqrt(jnp.mean(values * values, axis=-1, keepdims=True) + epsilon)


def norm_back(grad_normed, values, scale):
    inner = jnp.mean(grad_normed * values, axis=-1, keepdims=True)
    return scale * (grad_normed - values * scale * scale * inner)


def contract_rows(left, right):
    return lax.dot_general(
        left, right, (((0,), (0,)), ((), ())), preferred_element_type=jnp.float32
    )


def contract_cols(left, right):
    return lax.dot_general(
        left, right, (((1,), (1,)), ((), ())), preferred_element_type=jnp.float32
    )


def body(
    tokens, gain_first, w_in, conv_weight, w_out, gain_second, w_gate, w_up, w_down, cotangent
):
    shards = (gain_first, w_in, conv_weight, w_out, gain_second, w_gate, w_up, w_down)
    gathered = (
        lax.all_gather(shards[0], "fsdp", axis=0, tiled=True),
        lax.all_gather(shards[1], "fsdp", axis=0, tiled=True),
        lax.all_gather(shards[2], "fsdp", axis=0, tiled=True),
        lax.all_gather(shards[3], "fsdp", axis=0, tiled=True),
        lax.all_gather(shards[4], "fsdp", axis=0, tiled=True),
        lax.all_gather(shards[5], "fsdp", axis=0, tiled=True),
        lax.all_gather(shards[6], "fsdp", axis=0, tiled=True),
        lax.all_gather(shards[7], "fsdp", axis=0, tiled=True),
    )
    gain_one, in_full, conv_full, out_full, gain_two, gate_full, up_full, down_full = gathered
    model_width = tokens.shape[1]
    length = tokens.shape[0]
    inputs = tokens.astype(jnp.float32)
    scale_one = norm_scale(inputs)
    normed = (inputs * scale_one * gain_one.astype(jnp.float32)).astype(jnp.bfloat16)
    projected = jnp.dot(normed, in_full, preferred_element_type=jnp.float32)
    in_gate = projected[:, :model_width]
    out_gate = projected[:, model_width : 2 * model_width]
    carried = projected[:, 2 * model_width :]
    mixed = (in_gate * carried).astype(jnp.bfloat16)
    earlier = passed_along(mixed[length - 2 :], "fsdp", 1)
    extended = jnp.concatenate([earlier, mixed], 0).astype(jnp.float32)
    kernel = conv_full.astype(jnp.float32)
    convolved = (
        kernel[:, 0] * extended[2:]
        + kernel[:, 1] * extended[1 : length + 1]
        + kernel[:, 2] * extended[:length]
    )
    gated = (out_gate * convolved).astype(jnp.bfloat16)
    middle = inputs + jnp.dot(gated, out_full, preferred_element_type=jnp.float32)
    scale_two = norm_scale(middle)
    normed_two = (middle * scale_two * gain_two.astype(jnp.float32)).astype(jnp.bfloat16)
    gate_value = jnp.dot(normed_two, gate_full, preferred_element_type=jnp.float32)
    up_value = jnp.dot(normed_two, up_full, preferred_element_type=jnp.float32)
    sigmoid_gate = jax.nn.sigmoid(gate_value)
    silu_gate = gate_value * sigmoid_gate
    hidden = (silu_gate * up_value).astype(jnp.bfloat16)
    result = middle + jnp.dot(hidden, down_full, preferred_element_type=jnp.float32)
    back_weights = (
        lax.all_gather(shards[0], "fsdp", axis=0, tiled=True),
        lax.all_gather(shards[1], "fsdp", axis=0, tiled=True),
        lax.all_gather(shards[2], "fsdp", axis=0, tiled=True),
        lax.all_gather(shards[3], "fsdp", axis=0, tiled=True),
        lax.all_gather(shards[4], "fsdp", axis=0, tiled=True),
        lax.all_gather(shards[5], "fsdp", axis=0, tiled=True),
        lax.all_gather(shards[6], "fsdp", axis=0, tiled=True),
        lax.all_gather(shards[7], "fsdp", axis=0, tiled=True),
    )
    gain_back, in_back, conv_back, out_back, gain_two_back, gate_back, up_back, down_back = (
        back_weights
    )
    outer = cotangent.astype(jnp.float32)
    grad_down = contract_rows(hidden, cotangent)
    grad_hidden = contract_cols(cotangent, down_back)
    grad_gate = (
        grad_hidden * up_value * sigmoid_gate * (1.0 + gate_value * (1.0 - sigmoid_gate))
    ).astype(jnp.bfloat16)
    grad_upper = (grad_hidden * silu_gate).astype(jnp.bfloat16)
    grad_gate_w = contract_rows(normed_two, grad_gate)
    grad_up_w = contract_rows(normed_two, grad_upper)
    grad_normed_two = contract_cols(grad_gate, gate_back) + contract_cols(grad_upper, up_back)
    grad_gain_two = jnp.sum(grad_normed_two * middle * scale_two, axis=0)
    grad_middle = outer + norm_back(
        grad_normed_two * gain_two_back.astype(jnp.float32), middle, scale_two
    )
    grad_branch = grad_middle.astype(jnp.bfloat16)
    grad_out_w = contract_rows(gated, grad_branch)
    grad_gated = contract_cols(grad_branch, out_back)
    grad_out_gate = grad_gated * convolved
    grad_conv = grad_gated * out_gate
    grad_kernel = jnp.stack(
        [
            jnp.sum(grad_conv * extended[2:], axis=0),
            jnp.sum(grad_conv * extended[1 : length + 1], axis=0),
            jnp.sum(grad_conv * extended[:length], axis=0),
        ],
        axis=1,
    )
    kernel_back = conv_back.astype(jnp.float32)
    blank = jnp.zeros((2, model_width), jnp.float32)
    padded_grad = jnp.concatenate([blank, grad_conv, blank], 0)
    grad_extended = (
        kernel_back[:, 0] * padded_grad[: length + 2]
        + kernel_back[:, 1] * padded_grad[1 : length + 3]
        + kernel_back[:, 2] * padded_grad[2 : length + 4]
    )
    later_rows = passed_along(grad_extended[:2], "fsdp", -1)
    grad_mixed = grad_extended[2:] + jnp.concatenate(
        [jnp.zeros((length - 2, model_width), jnp.float32), later_rows], 0
    )
    grad_in_gate = grad_mixed * carried
    grad_carried = grad_mixed * in_gate
    grad_projected = jnp.concatenate([grad_in_gate, grad_out_gate, grad_carried], 1).astype(
        jnp.bfloat16
    )
    grad_in_w = contract_rows(normed, grad_projected)
    grad_normed = contract_cols(grad_projected, in_back)
    grad_gain_one = jnp.sum(grad_normed * inputs * scale_one, axis=0)
    grad_inputs = grad_middle + norm_back(
        grad_normed * gain_back.astype(jnp.float32), inputs, scale_one
    )
    shares = (
        lax.psum_scatter(grad_gain_one, "fsdp", scatter_dimension=0, tiled=True),
        lax.psum_scatter(grad_in_w, "fsdp", scatter_dimension=0, tiled=True),
        lax.psum_scatter(grad_kernel, "fsdp", scatter_dimension=0, tiled=True),
        lax.psum_scatter(grad_out_w, "fsdp", scatter_dimension=0, tiled=True),
        lax.psum_scatter(grad_gain_two, "fsdp", scatter_dimension=0, tiled=True),
        lax.psum_scatter(grad_gate_w, "fsdp", scatter_dimension=0, tiled=True),
        lax.psum_scatter(grad_up_w, "fsdp", scatter_dimension=0, tiled=True),
        lax.psum_scatter(grad_down, "fsdp", scatter_dimension=0, tiled=True),
    )
    totals = (
        lax.psum(shares[0].astype(jnp.bfloat16), "rep").astype(jnp.float32),
        lax.psum(shares[1].astype(jnp.bfloat16), "rep").astype(jnp.float32),
        lax.psum(shares[2].astype(jnp.bfloat16), "rep").astype(jnp.float32),
        lax.psum(shares[3].astype(jnp.bfloat16), "rep").astype(jnp.float32),
        lax.psum(shares[4].astype(jnp.bfloat16), "rep").astype(jnp.float32),
        lax.psum(shares[5].astype(jnp.bfloat16), "rep").astype(jnp.float32),
        lax.psum(shares[6].astype(jnp.bfloat16), "rep").astype(jnp.float32),
        lax.psum(shares[7].astype(jnp.bfloat16), "rep").astype(jnp.float32),
    )
    return (
        result.astype(jnp.bfloat16),
        grad_inputs,
        totals[0],
        totals[1],
        totals[2],
        totals[3],
        totals[4],
        totals[5],
        totals[6],
        totals[7],
    )


def solution(mesh):
    return jax.shard_map(
        body,
        mesh=mesh,
        in_specs=(
            P(("rep", "fsdp"), None),
            P("fsdp"),
            P("fsdp", None),
            P("fsdp", None),
            P("fsdp", None),
            P("fsdp"),
            P("fsdp", None),
            P("fsdp", None),
            P("fsdp", None),
            P(("rep", "fsdp"), None),
        ),
        out_specs=(
            P(("rep", "fsdp"), None),
            P(("rep", "fsdp"), None),
            P("fsdp"),
            P("fsdp", None),
            P("fsdp", None),
            P("fsdp", None),
            P("fsdp"),
            P("fsdp", None),
            P("fsdp", None),
            P("fsdp", None),
        ),
        check_vma=False,
    )
```

profile of v0, /device:TPU:1, one launch (start us, length us, event | category | flops | bytes accessed | tf_op | source)
XLA Modules:
  0.0 2480.4 jit_solution(10759914795723876644)
XLA Ops:
  7.2 0.7 all-gather.7.cloned.1.call-update
  8.0 0.7 all-gather.9.cloned.1.call-update
  8.7 0.7 all-gather.11.cloned.1.call-update
  9.4 0.5 all-gather.13.cloned.1.call-update
  10.0 0.5 all-gather.15.cloned.1.call-update
  10.6 1.3 fusion.28
  12.6 0.8 dynamic-update-slice
  13.4 0.8 dynamic-update-slice.1
  14.3 140.8 %all-reduce.8 = (bf16[1024]{0:T(1024)(128)(2,1)S(1)}, bf16[1024]{0:T(1024)(128)(2,1)S(1)}) all-reduce(bf16[1024]{0:T(1024)(128)(2,1)S(1)} %dynamic-update-slice, bf16[1024]{0:T(1024)(128)(2,1)S(1)} %dynamic-update-slice.1), channel_id=1, replica_groups=mesh['rep'=2,'fsdp'=64] {'fsdp'}, use_global_device_ids=true, to_apply=%add.3 | all-reduce | flops 2048 | bytes 8192
  155.1 81.8 %all-gather = bf16[64,16,3]{1,2,0:T(4,128)(2,1)S(1)} all-gather(bf16[1,16,3]{1,2,0:T(4,128)(2,1)} %bitcast.45), channel_id=1, replica_groups=mesh['rep'=2,'fsdp'=64] {'fsdp'}, dimensions={0}, use_global_device_ids=true | all-gather | bytes 6240 | tf_op jit(solution)/shard_map/all_gather | solution.py:43
  237.2 1.2 fusion.12
  238.5 4.9 fusion.23
  243.6 3.8 collective-permute-start
  247.4 0.5 collective-permute-done
  248.1 1.3 multiply_convert_fusion.7
  249.5 2.6 multiply_reduce_fusion.5
  252.3 88.1 %all-gather.11.cloned.1.call-done = bf16[1024,4608]{1,0:T(8,128)(2,1)} async-done(((bf16[16,4608]{1,0:T(8,128)(2,1)}), bf16[1024,4608]{1,0:T(8,128)(2,1)}) %all-gather.11.cloned.1.call-update) | async-done | bytes 9437200 | tf_op jit(solution)/shard_map/all_gather | solution.py:46
  340.4 7.9 fusion.29
  348.3 105.8 %all-gather.13.cloned.1.call-done = bf16[1024,4608]{1,0:T(8,128)(2,1)} async-done(((bf16[16,4608]{1,0:T(8,128)(2,1)}), bf16[1024,4608]{1,0:T(8,128)(2,1)}) %all-gather.13.cloned.1.call-update) | async-done | bytes 9437200 | tf_op jit(solution)/shard_map/all_gather | solution.py:47
  454.2 7.9 fusion.30
  462.1 106.2 %all-gather.15.cloned.1.call-done = bf16[4608,1024]{1,0:T(8,128)(2,1)} async-done(((bf16[72,1024]{1,0:T(8,128)(2,1)}), bf16[4608,1024]{1,0:T(8,128)(2,1)}) %all-gather.15.cloned.1.call-update) | async-done | bytes 9437200 | tf_op jit(solution)/shard_map/all_gather | solution.py:48
  568.3 9.9 multiply_convert_fusion
  578.2 6.9 fusion.31
  585.2 1.2 copy-done.2
  586.4 2.9 multiply_reduce_fusion
  589.3 1.7 multiply_add_fusion
  591.1 0.8 fusion.20
  592.3 0.6 multiply_reduce_fusion.3
  593.4 2.4 collective-permute-start.1
  595.8 2.6 collective-permute-done.1
  598.8 0.8 copy-done.16
  599.7 6.4 fusion.16
  606.2 9.6 fusion.32
  615.8 9.7 fusion.33
  625.6 1.0 copy-done.15
  626.5 9.6 fusion.34
  636.2 1.1 copy.24
  637.4 2.8 fusion.18
  641.4 7.9 fusion.1
  649.4 4.9 fusion.15
  654.2 138.4 %all-reduce.7 = (bf16[1024]{0:T(1024)(128)(2,1)S(1)}, bf16[1024]{0:T(1024)(128)(2,1)S(1)}) all-reduce(f32[1024]{0:T(1024)S(1)} %get-tuple-element.15, f32[1024]{0:T(1024)S(1)} %get-tuple-element.13), channel_id=2, replica_groups=mesh['rep'=2,'fsdp'=64] {'fsdp'}, use_global_device_ids=true, to_apply=%region_5.0.clone | all-reduce | flops 2048 | bytes 12288
  792.8 115.6 %reduce-scatter.9.cloned.1.call-done = f32[16,3072]{1,0:T(8,128)} async-done(((f32[1024,3072]{1,0:T(8,128)}), f32[16,3072]{1,0:T(8,128)}) %reduce-scatter.9.cloned.1.call-update) | async-done | bytes 196624 | tf_op jit(solution)/shard_map/reduce_scatter | solution.py:144
  908.4 1.6 convert_element_type.114
  910.0 312.5 %reduce-scatter.13.cloned.1.call-done = f32[16,4608]{1,0:T(8,128)} async-done(((f32[1024,4608]{1,0:T(8,128)}), f32[16,4608]{1,0:T(8,128)}) %reduce-scatter.13.cloned.1.call-update) | async-done | bytes 294928 | tf_op jit(solution)/shard_map/reduce_scatter | solution.py:148
  1222.5 1.6 convert_element_type.122
  1224.1 312.7 %reduce-scatter.15.cloned.1.call-done = f32[16,4608]{1,0:T(8,128)} async-done(((f32[1024,4608]{1,0:T(8,128)}), f32[16,4608]{1,0:T(8,128)}) %reduce-scatter.15.cloned.1.call-update) | async-done | bytes 294928 | tf_op jit(solution)/shard_map/reduce_scatter | solution.py:149
  1536.8 1.6 convert_element_type.124
  1538.4 312.7 %reduce-scatter.17.cloned.1.call-done = f32[72,1024]{1,0:T(8,128)} async-done(((f32[4608,1024]{1,0:T(8,128)}), f32[72,1024]{1,0:T(8,128)}) %reduce-scatter.17.cloned.1.call-update) | async-done | bytes 294928 | tf_op jit(solution)/shard_map/reduce_scatter | solution.py:150
  1851.1 1.6 convert_element_type.126
  1852.8 281.9 %reduce-scatter.19.cloned.1.call-done = f32[16,3]{1,0:T(8,128)} async-done(((f32[1024,3]{1,0:T(8,128)}), f32[16,3]{1,0:T(8,128)}) %reduce-scatter.19.cloned.1.call-update) | async-done | bytes 208
  2134.6 0.8 copy.25
  2135.4 287.5 %reduce-scatter.11.cloned.1.call-done = f32[16,1024]{1,0:T(8,128)} async-done(((f32[1024,1024]{1,0:T(8,128)}), f32[16,1024]{1,0:T(8,128)}) %reduce-scatter.11.cloned.1.call-update) | async-done | bytes 65552 | tf_op jit(solution)/shard_map/reduce_scatter | solution.py:146
  2423.0 0.8 convert_element_type.118
  2423.8 1.3 fusion.11
  2425.1 10.4 all-reduce.9
  2435.5 0.6 convert_element_type.119
  2436.1 0.6 convert_element_type.117
  2436.7 0.5 convert_element_type.113
  2437.2 0.5 convert_element_type.121
  2437.7 29.3 %all-reduce.13.cloned.1.call-done = (bf16[16,3072]{1,0:T(8,128)(2,1)}, bf16[16,4608]{1,0:T(8,128)(2,1)}, bf16[16,4608]{1,0:T(8,128)(2,1)}, bf16[72,1024]{1,0:T(8,128)(2,1)}) async-done(((bf16[16,3072]{1,0:T(8,128)(2,1)}, bf16[16,4608]{1,0:T(8,128)(2,1)}, bf16[16,4608]{1,0:T(8,128)(2,1)}, bf16[72,1024]{1,0:T(8,128)(2,1)}), (bf16[16,3072]{1,0:T(8,128)(2,1)}, bf16[16,4608]{1,0:T(8,128)(2,1)}, ...) | async-done | bytes 540688 | tf_op jit(solution)/shard_map/psum | solution.py:154
  2467.0 1.6 convert_element_type.123
  2468.7 1.6 convert_element_type.125
  2470.3 1.6 convert_element_type.127
  2471.9 1.6 convert_element_type.115
  (81 shorter events, 3.5 us)
Async XLA Ops:
  7.2 231.3 %all-gather.7.cloned.1.call-start = ((), (), s32[]{:S(2)}) async-start(), calls=%async_computation.6 | async-start | bytes 6389760 | tf_op jit(solution)/shard_map/all_gather | solution.py:42
  7.9 241.6 %all-gather.9.cloned.1.call-start = ((), (), s32[]{:S(2)}) async-start(), calls=%async_computation.7 | async-start | bytes 2129920 | tf_op jit(solution)/shard_map/all_gather | solution.py:44
  8.7 331.7 %all-gather.11.cloned.1.call-start = ((), (), s32[]{:S(2)}) async-start(), calls=%async_computation.8 | async-start | bytes 9584640 | tf_op jit(solution)/shard_map/all_gather | solution.py:46
  9.4 444.8 %all-gather.13.cloned.1.call-start = ((), (), s32[]{:S(2)}) async-start(), calls=%async_computation.9 | async-start | bytes 9584640 | tf_op jit(solution)/shard_map/all_gather | solution.py:47
  10.0 558.3 %all-gather.15.cloned.1.call-start = ((), (), s32[]{:S(2)}) async-start(), calls=%async_computation.10 | async-start | bytes 9584640 | tf_op jit(solution)/shard_map/all_gather | solution.py:48
  10.6 897.8 %reduce-scatter.9.cloned.1.call-start = ((), (), s32[]{:S(2)}) async-start(), calls=%async_computation.11 | async-start | bytes 12779520 | tf_op jit(solution)/shard_map/reduce_scatter | solution.py:144
  243.4 4.7 copy-start
  243.6 4.4 collective-permute-start
  248.1 1.4 copy-start.6
  249.5 2.6 copy-start.7
  252.1 333.1 %copy-start.3 = (f32[256,1024]{1,0:T(8,128)}, f32[256,1024]{1,0:T(8,128)S(1)}, u32[]{:S(2)}) copy-start(f32[256,1024]{1,0:T(8,128)S(1)} %get-tuple-element.44) | copy-start | bytes 3145732
  578.2 7.0 copy-start.11
  578.2 7.0 copy-start.10
  578.2 8.1 copy-start.2
  586.4 2.9 copy-start.14
  589.2 1.9 copy-start.5
  589.3 2.8 copy-start.1
  589.3 3.1 copy-start.9
  593.0 5.7 copy-start.12
  593.4 5.0 collective-permute-start.1
  598.7 0.8 copy-start.16
  598.7 1.0 copy-start.18
  606.1 616.4 %reduce-scatter.13.cloned.1.call-start = ((), (), s32[]{:S(2)}) async-start(), calls=%async_computation.13 | async-start | bytes 19169280 | tf_op jit(solution)/shard_map/reduce_scatter | solution.py:148
  615.8 921.0 %reduce-scatter.15.cloned.1.call-start = ((), (), s32[]{:S(2)}) async-start(), calls=%async_computation.14 | async-start | bytes 19169280 | tf_op jit(solution)/shard_map/reduce_scatter | solution.py:149
  625.5 1.0 copy-start.15
  625.5 1225.6 %reduce-scatter.17.cloned.1.call-start = ((), (), s32[]{:S(2)}) async-start(), calls=%async_computation.15 | async-start | bytes 19169280 | tf_op jit(solution)/shard_map/reduce_scatter | solution.py:150
  636.1 1.3 copy-start.8
  636.2 1498.5 %reduce-scatter.19.cloned.1.call-start = ((), (), s32[]{:S(2)}) async-start(), calls=%async_computation.16 | async-start | bytes 532480
  637.3 1785.6 %reduce-scatter.11.cloned.1.call-start = ((), (), s32[]{:S(2)}) async-start(), calls=%async_computation.12 | async-start | bytes 4259840 | tf_op jit(solution)/shard_map/reduce_scatter | solution.py:146
  640.2 1.2 copy-start.4
  640.2 1826.8 %all-reduce.13.cloned.1.call-start = ((), (), s32[]{:S(2)}) async-start(), calls=%async_computation.17 | async-start | bytes 1081344 | tf_op jit(solution)/shard_map/psum | solution.py:154
  641.4 8.0 copy-start.13
  641.4 8.0 copy-start.17
  641.4 8.0 copy-start.19
Sparse Core Ops, SparseCore 0:
  9.7 112.2 all-gather.6
  123.8 102.3 all-gather.8
  227.9 112.4 all-gather.10
  342.0 112.1 all-gather.12
  455.7 112.5 all-gather.14
  606.2 302.0 reduce-scatter.8
  910.8 311.6 reduce-scatter.12
  1224.9 311.8 reduce-scatter.14
  1539.2 311.8 reduce-scatter.16
  1853.3 281.2 reduce-scatter.18
  2137.1 285.7 reduce-scatter.10
  2426.6 40.3 all-reduce.12
where the time goes:
time: 2480 us
  waiting for transfers between devices  1960 us (79%)
  blocking collectives  371 us (15%)
  matrix products  94.7 us (4%)
    reduce_scatter x1, waiting for transfers between devices, body(): lax.psum_scatter(grad_down, 'fsdp', scatter_dimension=0, tiled=True)  313 us
    reduce_scatter x1, waiting for transfers between devices, body(): lax.psum_scatter(grad_up_w, 'fsdp', scatter_dimension=0, tiled=True)  313 us
    reduce_scatter x1, waiting for transfers between devices, body(): lax.psum_scatter(grad_gate_w, 'fsdp', scatter_dimension=0, tiled=True)  313 us
    reduce_scatter x1, waiting for transfers between devices, body(): lax.psum_scatter(grad_out_w, 'fsdp', scatter_dimension=0, tiled=True)  288 us
    unnamed x13, waiting for transfers between devices  285 us
    unnamed x2, blocking collectives  279 us
    reduce_scatter x1, waiting for transfers between devices, body(): lax.psum_scatter(grad_in_w, 'fsdp', scatter_dimension=0, tiled=True)  116 us
    all_gather x1, waiting for transfers between devices, body(): lax.all_gather(shards[7], 'fsdp', axis=0, tiled=True)  106 us
  transfers between devices with their start and end apart: 14, of which 12 were waited for; matrix products, arithmetic and copies ran while one was open for 4% of the time, Pallas kernels for 0%

commit v1 on v0

v1 whole, which is shorter than its diff:
```python
import jax
import jax.numpy as jnp
from jax import lax
from jax.sharding import PartitionSpec as P

epsilon = 1e-05

SIDE = 4
PLANE = SIDE * SIDE
HALF = PLANE * 2


def place(z, plane, core):
    return (z * PLANE + plane) * 2 + core


def moves(target):
    return [
        (place(z, plane, core), place(*target(z, plane, core)))
        for z in range(2)
        for plane in range(PLANE)
        for core in range(2)
    ]


TO_CORE = moves(lambda z, plane, core: (z, plane, 1 - core))
TO_Z = moves(lambda z, plane, core: (1 - z, plane, core))
TO_NEXT = moves(lambda z, plane, core: (z, (plane + 1) % PLANE, core))
TO_PREVIOUS = moves(lambda z, plane, core: (z, (plane - 1) % PLANE, core))
TEAMS = [
    [place(z, plane, core) for z in range(2) for core in range(2)] for plane in range(PLANE)
]
PLANES = [
    [place(z, plane, core) for plane in range(PLANE)] for z in range(2) for core in range(2)
]
BOTH_TEAMS = [[rep * 2 * HALF + member for rep in range(2) for member in team] for team in TEAMS]


def to_core(value):
    return lax.ppermute(value, "fsdp", TO_CORE)


def to_z(value):
    return lax.ppermute(value, "fsdp", TO_Z)


def norm_scale(values):
    return lax.rsqrt(jnp.mean(values * values, axis=-1, keepdims=True) + epsilon)


def norm_back(grad_normed, values, scale):
    inner = jnp.mean(grad_normed * values, axis=-1, keepdims=True)
    return scale * (grad_normed - values * scale * scale * inner)


def contract_rows(left, right):
    return lax.dot_general(
        left, right, (((0,), (0,)), ((), ())), preferred_element_type=jnp.float32
    )


def contract_cols(left, right):
    return lax.dot_general(
        left, right, (((1,), (1,)), ((), ())), preferred_element_type=jnp.float32
    )


def by_member(shard, parts):
    rows, columns = shard.shape
    width = columns // (parts * 2 * HALF)
    split = shard.reshape(rows, parts, 2, PLANE, 2, width)
    return split.transpose(2, 4, 0, 1, 3, 5).reshape(4, rows, columns // 4)


def from_members(blocks, parts):
    members, rows, columns = blocks.shape
    width = columns // (parts * PLANE)
    split = blocks.reshape(2, 2, rows, parts, PLANE, width)
    return split.transpose(2, 3, 0, 4, 1, 5).reshape(rows, 4 * columns)


def team_swap(blocks):
    return lax.all_to_all(blocks, "fsdp", 0, 0, tiled=True, axis_index_groups=TEAMS)


def plane_gather(value, axis):
    return lax.all_gather(value, "fsdp", axis=axis, tiled=True, axis_index_groups=PLANES)


def plane_scatter(value, axis):
    return lax.psum_scatter(
        value, "fsdp", scatter_dimension=axis, tiled=True, axis_index_groups=PLANES
    )


def gather_rows(blocks):
    members, rows, columns = blocks.shape
    return plane_gather(blocks.reshape(2, 2 * rows, columns), 1).reshape(-1, columns)


def scatter_rows(value):
    total, columns = value.shape
    shared = plane_scatter(value.reshape(2, total // 2, columns), 1)
    return shared.reshape(4, -1, columns)


def team_tokens(own):
    pair = jnp.stack([own, to_z(own)])
    return with_core(pair)


def with_core(pair):
    other = to_core(pair)
    return jnp.stack([pair[0], other[0], pair[1], other[1]])


def core_sum(partial):
    sent = jnp.stack([partial[1], partial[3]]).astype(jnp.bfloat16)
    return jnp.stack([partial[0], partial[2]]) + to_core(sent).astype(jnp.float32)


def team_sum(partial):
    pair = core_sum(partial)
    other = to_z(pair.astype(jnp.bfloat16)).astype(jnp.float32)
    return pair + other[::-1]


def own_sum(partial):
    pair = core_sum(partial)
    return pair[0] + to_z(pair[1].astype(jnp.bfloat16)).astype(jnp.float32)


def body(
    tokens, gain_first, w_in, conv_weight, w_out, gain_second, w_gate, w_up, w_down, cotangent
):
    low, wide = jnp.bfloat16, jnp.float32
    length, model_width = tokens.shape
    position = lax.axis_index("fsdp")
    core, plane, z = position % 2, position // 2 % PLANE, position // HALF
    rows = w_in.shape[0]
    channels = model_width // 4

    gains = jnp.pad(jnp.stack([gain_first, gain_second], 1), ((0, 0), (0, 126)))
    in_pack = jnp.concatenate(
        [by_member(w_in, 3), jnp.broadcast_to(gains, (4,) + gains.shape)], 2
    )
    in_all = gather_rows(team_swap(in_pack))
    out_pack = jnp.concatenate([w_out, jnp.pad(conv_weight, ((0, 0), (0, 125)))], 1)
    out_all = plane_gather(out_pack, 0)
    ff_pack = team_swap(jnp.concatenate([by_member(w_gate, 1), by_member(w_up, 1)], 2))
    ff_all = gather_rows(ff_pack)
    down_full = plane_gather(w_down, 0)

    in_full = in_all[:, : 3 * channels]
    gain_one = in_all[:, 3 * channels].astype(wide)
    gain_two = in_all[:, 3 * channels + 1].astype(wide)
    out_full = out_all[:, :model_width]
    kernel = out_all[:, model_width : model_width + 3].astype(wide).T
    units = ff_all.shape[1] // 2
    gate_full, up_full = ff_all[:, :units], ff_all[:, units:]

    team_inputs = team_tokens(tokens)
    team_outer = team_tokens(cotangent)
    outer_flat = team_outer.reshape(4 * length, model_width)

    inputs = team_inputs.astype(wide)
    scale_one = norm_scale(inputs)
    normed = (inputs * scale_one * gain_one).astype(low).reshape(4 * length, model_width)
    projected = jnp.dot(normed, in_full, preferred_element_type=wide)
    in_gate = projected[:, :channels].reshape(4, length, channels)
    out_gate = projected[:, channels : 2 * channels].reshape(4, length, channels)
    carried = projected[:, 2 * channels :].reshape(4, length, channels)
    mixed = (in_gate * carried).astype(low)

    def by_core(first, second):
        return jnp.where(core == 0, first, second)

    tails = mixed[:, length - 2 :]
    sent = by_core(tails[1::2], tails[0::2])
    received = lax.ppermute(sent, "fsdp", TO_NEXT)
    nothing = jnp.zeros_like(received[0])
    shifted = jnp.where(
        z == 0, jnp.stack([nothing, received[0]]), jnp.stack([received[1], nothing])
    )
    before = jnp.where(plane == 0, shifted, received)
    own_before = by_core(before, tails[1::2])
    other_before = by_core(tails[0::2], before)
    earlier = jnp.stack([own_before[0], other_before[0], own_before[1], other_before[1]])
    extended = jnp.concatenate([earlier, mixed], 1).astype(wide)
    lagged = (extended[:, 2:], extended[:, 1 : length + 1], extended[:, :length])
    convolved = kernel[0] * lagged[0] + kernel[1] * lagged[1] + kernel[2] * lagged[2]
    gated = (out_gate * convolved).astype(low).reshape(4 * length, channels)
    branch = jnp.dot(gated, out_full, preferred_element_type=wide)
    middle = jnp.stack([inputs[0], inputs[2]]) + team_sum(
        branch.reshape(4, length, model_width)
    )
    scale_two = norm_scale(middle)
    normed_two = with_core((middle * scale_two * gain_two).astype(low))
    normed_two = normed_two.reshape(4 * length, model_width)
    gate_value = jnp.dot(normed_two, gate_full, preferred_element_type=wide)
    up_value = jnp.dot(normed_two, up_full, preferred_element_type=wide)
    sigmoid_gate = jax.nn.sigmoid(gate_value)
    silu_gate = gate_value * sigmoid_gate
    hidden = (silu_gate * up_value).astype(low)

    grad_hidden = contract_cols(outer_flat, down_full)
    grad_gate = (
        grad_hidden * up_value * sigmoid_gate * (1.0 + gate_value * (1.0 - sigmoid_gate))
    ).astype(low)
    grad_upper = (grad_hidden * silu_gate).astype(low)
    grad_down = contract_rows(hidden, outer_flat).astype(low)
    grad_gate_w = contract_rows(normed_two, grad_gate).astype(low)
    grad_up_w = contract_rows(normed_two, grad_upper).astype(low)
    down_share = plane_scatter(grad_down, 0)
    ff_share = scatter_rows(jnp.concatenate([grad_gate_w, grad_up_w], 1))

    grad_normed_two = contract_cols(grad_gate, gate_full) + contract_cols(grad_upper, up_full)
    grad_normed_two = team_sum(grad_normed_two.reshape(4, length, model_width))
    grad_gain_two = jnp.sum(grad_normed_two[0] * middle[0] * scale_two[0], axis=0)
    outer = jnp.stack([team_outer[0], team_outer[2]]).astype(wide)
    grad_middle = outer + norm_back(grad_normed_two * gain_two, middle, scale_two)
    grad_branch = with_core(grad_middle.astype(low)).reshape(4 * length, model_width)

    down_term = jnp.dot(hidden, down_full, preferred_element_type=wide)
    result = middle[0] + own_sum(down_term.reshape(4, length, model_width))

    grad_out_w = contract_rows(gated, grad_branch)
    grad_gated = contract_cols(grad_branch, out_full).reshape(4, length, channels)
    grad_out_gate = grad_gated * convolved
    grad_conv = grad_gated * out_gate
    grad_kernel = jnp.stack([jnp.sum(grad_conv * rows_of, axis=(0, 1)) for rows_of in lagged], 1)

    heads = grad_conv[:, :2]
    sent = by_core(heads[0::2], heads[1::2])
    received = lax.ppermute(sent, "fsdp", TO_PREVIOUS)
    nothing = jnp.zeros_like(received[0])
    shifted = jnp.where(
        z == 0, jnp.stack([received[1], nothing]), jnp.stack([nothing, received[0]])
    )
    after = jnp.where(plane == PLANE - 1, shifted, received)
    own_after = by_core(heads[1::2], after)
    other_after = by_core(after, heads[0::2])
    later = jnp.stack([own_after[0], other_after[0], own_after[1], other_after[1]])
    grad_long = jnp.concatenate([grad_conv, later], 1)
    grad_mixed = (
        kernel[0] * grad_long[:, :length]
        + kernel[1] * grad_long[:, 1 : length + 1]
        + kernel[2] * grad_long[:, 2:]
    )
    grad_projected = jnp.concatenate(
        [
            (grad_mixed * carried).astype(low),
            grad_out_gate.astype(low),
            (grad_mixed * in_gate).astype(low),
        ],
        2,
    ).reshape(4 * length, 3 * channels)
    grad_in_w = contract_rows(normed, grad_projected)
    grad_normed = contract_cols(grad_projected, in_full).reshape(4, length, model_width)
    grad_gain_one = jnp.sum(grad_normed * inputs * scale_one, axis=(0, 1))

    in_grads = jnp.concatenate(
        [
            grad_in_w,
            jnp.pad(jnp.stack([grad_gain_one, grad_gain_two], 1), ((0, 0), (0, 126))),
        ],
        1,
    ).astype(low)
    out_grads = jnp.concatenate(
        [grad_out_w, jnp.pad(grad_kernel, ((0, 0), (0, 125)))], 1
    ).astype(low)
    in_share = scatter_rows(in_grads)
    out_share = plane_scatter(out_grads, 0)

    grad_normed_own = own_sum(grad_normed)
    grad_inputs = grad_middle[0] + norm_back(
        grad_normed_own * gain_one, inputs[0], scale_one[0]
    )

    def all_reps(blocks):
        swapped = lax.all_to_all(
            jnp.concatenate([blocks, blocks]),
            ("rep", "fsdp"),
            0,
            0,
            tiled=True,
            axis_index_groups=BOTH_TEAMS,
        )
        return swapped[:4].astype(wide) + swapped[4:].astype(wide)

    def both_reps(value):
        other = lax.ppermute(value, "rep", [(0, 1), (1, 0)])
        return value.astype(wide) + other.astype(wide)

    in_total = all_reps(in_share)
    ff_total = all_reps(ff_share)
    out_total = both_reps(out_share)
    down_total = both_reps(down_share)
    gain_total = jnp.sum(in_total[:, :, 3 * channels : 3 * channels + 2], axis=0)

    return (
        result.astype(low),
        grad_inputs,
        gain_total[:, 0],
        from_members(in_total[:, :, : 3 * channels], 3),
        out_total[:, model_width : model_width + 3],
        out_total[:, :model_width],
        gain_total[:, 1],
        from_members(ff_total[:, :, :units], 1),
        from_members(ff_total[:, :, units:], 1),
        down_total,
    )


def solution(mesh):
    return jax.shard_map(
        body,
        mesh=mesh,
        in_specs=(
            P(("rep", "fsdp"), None),
            P("fsdp"),
            P("fsdp", None),
            P("fsdp", None),
            P("fsdp", None),
            P("fsdp"),
            P("fsdp", None),
            P("fsdp", None),
            P("fsdp", None),
            P(("rep", "fsdp"), None),
        ),
        out_specs=(
            P(("rep", "fsdp"), None),
            P(("rep", "fsdp"), None),
            P("fsdp"),
            P("fsdp", None),
            P("fsdp", None),
            P("fsdp", None),
            P("fsdp"),
            P("fsdp", None),
            P("fsdp", None),
            P("fsdp", None),
        ),
        check_vma=False,
    )
```

time: 2480 us -> 590 us (0.24)
  waiting for transfers between devices: 1960 us -> 338 us
  blocking collectives: 371 us -> 29.3 us
  starting transfers between devices: 6.7 us -> 47.4 us
  matrix products: 94.7 us -> 57.9 us
  local copies, waits for them, and re-layouts: 9.46 us -> 45.2 us
    reduce_scatter x5 -> x2, waiting for transfers between devices: 1340 us -> 142 us  [plane_scatter(): lax.psum_scatter(value, 'fsdp', scatter_dimension=axis, tiled=True, axis_...]
    all_gather x5 -> x3, waiting for transfers between devices: 300 us -> 18.8 us  [plane_gather(): lax.all_gather(value, 'fsdp', axis=axis, tiled=True, axis_index_groups=PL...]
    unnamed x2 -> x0, blocking collectives: 279 us -> none
    unnamed x13 -> x9, waiting for transfers between devices: 285 us -> 91.9 us
    ppermute x2 -> x18, waiting for transfers between devices: 3.08 us -> 84.3 us  [the longest x6 76.2 us: to_z(): return lax.ppermute(value, 'fsdp', TO_Z)]
    all_gather x1, blocking collectives: 81.8 us -> 21.1 us  [plane_gather(): lax.all_gather(value, 'fsdp', axis=axis, tiled=True, axis_index_groups=PL...]
    psum x1 -> x0, waiting for transfers between devices: 29.3 us -> none  [body(): lax.psum(shares[1].astype(jnp.bfloat16), 'rep').astype(jnp.float32)]
  transfers between devices with their start and end apart: 14 -> 28, of which waited for: 12 -> 15; matrix products, arithmetic and copies ran while one was open for 4% -> 19% of each run, Pallas kernels for 0% -> 0%
where the time goes in v1:
time: 590 us; the launch traced here: 581 us
  waiting for transfers between devices  338 us (57%)
  matrix products  57.9 us (10%)
  starting transfers between devices  47.4 us (8%)
  other arithmetic  46.3 us (8%)
  local copies, waits for them, and re-layouts  45.2 us (8%)
  blocking collectives  29.3 us (5%)
  between operations  16.4 us (3%)
    reduce_scatter x2, waiting for transfers between devices, plane_scatter(): lax.psum_scatter(value, 'fsdp', scatter_dimension=axis, tiled=True, axis_...  142 us
    unnamed x9, waiting for transfers between devices  91.9 us
    ppermute x6, waiting for transfers between devices, to_z(): return lax.ppermute(value, 'fsdp', TO_Z)  76.2 us
    all_gather x1, blocking collectives, plane_gather(): lax.all_gather(value, 'fsdp', axis=axis, tiled=True, axis_index_groups=PL...  21.1 us
    dot_general x5, matrix products, contract_cols(): lax.dot_general(left, right, (((1,), (1,)), ((), ())), preferred_element_...  20 us
    dot_general x5, matrix products, contract_rows(): lax.dot_general(left, right, (((0,), (0,)), ((), ())), preferred_element_...  19.2 us
    all_gather x3, waiting for transfers between devices, plane_gather(): lax.all_gather(value, 'fsdp', axis=axis, tiled=True, axis_index_groups=PL...  18.8 us
    all_to_all x2, starting transfers between devices, all_reps(): lax.all_to_all(jnp.concatenate([blocks, blocks]), ('rep', 'fsdp'), 0, 0,...  13.7 us
  transfers between devices with their start and end apart: 28, of which 15 were waited for; matrix products, arithmetic and copies ran while one was open for 19% of the time, Pallas kernels for 0%

profile of v1, /device:TPU:1, one launch (start us, length us, event | category | flops | bytes accessed | tf_op | source)
XLA Modules:
  0.0 580.9 jit_solution(9942588843747779085)
XLA Ops:
  7.3 1.5 reshape.230
  9.8 8.2 %all_to_all.20 = bf16[4,16,896]{2,1,0:T(8,128)(2,1)} all-to-all(bf16[4,16,896]{2,1,0:T(8,128)(2,1)S(1)} %pad_maximum_fusion.18), channel_id=1, replica_groups={{0,1,32,33},{2,3,34,35},{4,5,36,37},{6,7,38,39},{8,9,40,41},{10,11,42,4..., dimensions={0} | all-to-all | bytes 229376 | tf_op jit(solution)/shard_map/all_to_all | solution.py:83
  19.3 11.9 %collective-permute-done = bf16[256,1024]{1,0:T(8,128)(2,1)S(1)} collective-permute-done((bf16[256,1024]{1,0:T(8,128)(2,1)S(1)}, bf16[256,1024]{1,0:T(8,128)(2,1)S(1)}, u32[]{:S(2)}, u32[]{:S(2)}) %collective-permute-start) | collective-permute-done | bytes 524320 | tf_op jit(solution)/shard_map/ppermute | solution.py:44
  32.4 1.9 collective-permute-start.1
  36.8 3.4 all-to-all-start.1
  40.4 21.1 %all_gather.13 = bf16[256,1152]{1,0:T(8,128)(2,1)S(1)} all-gather(bf16[16,1152]{1,0:T(8,128)(2,1)S(1)} %fusion.52), channel_id=1, replica_groups={{0,2,4,6,8,10,12,14,16,18,20,22,24,26,28,30},{1,3,5,7,9,11,13,15,17,19,..., dimensions={0}, use_global_device_ids=true | all-gather | bytes 626688 | tf_op jit(solution)/shard_map/all_gather | solution.py:87
  64.9 2.0 slice_convert_fusion.2
  67.1 2.2 fusion.2
  69.4 1.8 fusion.19
  74.9 4.6 collective-permute-done.2
  80.7 2.6 multiply_convert_fusion.11
  84.3 5.1 collective-permute-start.3
  90.9 11.4 %collective-permute-done.8 = bf16[256,1024]{1,0:T(8,128)(2,1)S(1)} collective-permute-done((bf16[256,1024]{1,0:T(8,128)(2,1)S(1)}, bf16[256,1024]{1,0:T(8,128)(2,1)S(1)}, u32[]{:S(2)}, u32[]{:S(2)}) %collective-permute-start.8) | collective-permute-done | bytes 524320 | tf_op jit(solution)/shard_map/ppermute | solution.py:44
  102.3 2.1 collective-permute-start.9
  104.7 1.4 fusion.26
  109.7 1.4 fusion.59
  111.6 20.1 %collective-permute-done.4 = bf16[2,256,1024]{2,1,0:T(8,128)(2,1)} collective-permute-done((bf16[2,256,1024]{2,1,0:T(8,128)(2,1)}, bf16[2,256,1024]{2,1,0:T(8,128)(2,1)}, u32[]{:S(2)}, u32[]{:S(2)}) %collective-permute-start.4) | collective-permute-done | bytes 1048608 | tf_op jit(solution)/shard_map/ppermute | solution.py:44
  131.7 1.5 convert_element_type.177
  133.2 2.5 multiply_reduce_fusion.2
  137.9 1.7 pad_maximum_fusion.3
  139.6 7.4 %fusion.77 = f32[1024,1152]{1,0:T(8,128)} fusion(bf16[1024,1024]{1,0:T(8,128)(2,1)} %bitcast.217, bf16[1152,1024]{1,0:T(8,128)(2,1)} %all-gather.8.cloned.1.call-done), kind=kOutput, calls=%fused_computation.187 | convolution fusion | flops 2415919104 | bytes 9175040 | tf_op jit(solution)/shard_map/dot_general | solution.py:63
  149.6 1.6 pad_maximum_fusion.2
  151.2 18.2 %all-gather.6.cloned.1.call-done = bf16[2,512,2304]{2,1,0:T(8,128)(2,1)} async-done(((bf16[2,32,2304]{2,1,0:T(8,128)(2,1)}), bf16[2,512,2304]{2,1,0:T(8,128)(2,1)}) %all-gather.6.cloned.1.call-update) | async-done | bytes 4718608 | tf_op jit(solution)/shard_map/all_gather | solution.py:87
  169.4 5.3 fusion.10
  174.7 6.4 %multiply_convert_fusion.1 = (bf16[1024,1152]{1,0:T(8,128)(2,1)S(1)}, bf16[1024,1152]{1,0:T(8,128)(2,1)S(1)}, bf16[1024,1152]{1,0:T(8,128)(2,1)S(1)}) fusion(f32[1024,1152]{1,0:T(8,128)} %fusion.77, f32[1024,1152]{1,0:T(8,128)S(1)} %fusion.10, bf16[1024,1024]{1,0:T(8,128)(2,1)S(1)} %bitcast.214, bf16[1024,2304]{1,0:T(8,128)(2,1)S(1)} %bitcast.245), kind=kOutput, calls=%fused_computation.2 | convolution fusion | flops 2433613824 | bytes 20971520 | tf_op jit(solution)/shard_map/dot_general | solution.py:200
  181.2 2.9 fusion.8
  184.1 2.9 fusion.75
  188.2 2.0 collective-permute-done.10
  190.6 1.5 collective-permute-start.11
  192.2 23.1 %collective-permute-done.11 = bf16[2,256,1024]{2,1,0:T(8,128)(2,1)S(1)} collective-permute-done((bf16[2,256,1024]{2,1,0:T(8,128)(2,1)S(1)}, bf16[2,256,1024]{2,1,0:T(8,128)(2,1)S(1)}, u32[]{:S(2)}, u32[]{:S(2)}) %collective-permute-start.11) | collective-permute-done | bytes 1048608 | tf_op jit(solution)/shard_map/ppermute | solution.py:44
  216.7 2.0 fusion.58
  219.9 4.4 fusion.76
  226.5 1.5 fusion.23
  228.4 2.1 multiply_reduce_fusion.5
  230.6 1.9 fusion.43
  232.6 6.4 %convolution_convert_fusion = bf16[1152,1024]{1,0:T(8,128)(2,1)} fusion(bf16[1024,1152]{1,0:T(8,128)(2,1)} %copy-done.63, bf16[1024,1024]{1,0:T(8,128)(2,1)} %bitcast.218), kind=kOutput, calls=%fused_computation.14 | convolution fusion | flops 2417098752 | bytes 6815744 | tf_op jit(solution)/shard_map/dot_general | solution.py:57
  239.1 1.8 slice_bitcast_fusion.9
  240.9 1.8 maximum_add_fusion.2
  246.2 2.9 collective-permute-start.13
  249.1 9.7 %collective-permute-done.7 = bf16[256,1024]{1,0:T(8,128)(2,1)} collective-permute-done((bf16[256,1024]{1,0:T(8,128)(2,1)}, bf16[256,1024]{1,0:T(8,128)(2,1)}, u32[]{:S(2)}, u32[]{:S(2)}) %collective-permute-start.7) | collective-permute-done | bytes 524320 | tf_op jit(solution)/shard_map/ppermute | solution.py:44
  258.9 2.7 fusion.29
  266.2 4.7 fusion.4
  271.3 3.0 bitcast_convert_fusion
  276.6 5.0 convolution_convert_fusion.1
  281.6 3.2 convolution_convert_fusion.2
  284.8 2.5 pad_maximum_fusion
  290.8 1.7 slice_bitcast_fusion.3
  294.2 21.2 %all-reduce.12.cloned.1.call-done = bf16[256,1152]{1,0:T(8,128)(2,1)} async-done(((bf16[256,1152]{1,0:T(8,128)(2,1)}), bf16[256,1152]{1,0:T(8,128)(2,1)}) %all-reduce.12.cloned.1.call-update) | async-done | bytes 589840
  316.2 2.9 collective-permute-start.16
  319.1 1.4 collective-permute-done.16
  322.6 69.9 %reduce-scatter.10.cloned.1.call-done = bf16[72,1024]{1,0:T(8,128)(2,1)} async-done(((bf16[1152,1024]{1,0:T(8,128)(2,1)}), bf16[72,1024]{1,0:T(8,128)(2,1)}) %reduce-scatter.10.cloned.1.call-update) | async-done | bytes 147472
  392.5 2.9 collective-permute-start.17
  395.3 1.5 fusion.42
  396.8 2.6 fusion.34
  399.4 69.3 %reduce-scatter.6.cloned.1.call-done = bf16[2,32,896]{2,1,0:T(8,128)(2,1)} async-done(((bf16[2,512,896]{2,1,0:T(8,128)(2,1)}), bf16[2,32,896]{2,1,0:T(8,128)(2,1)}) %reduce-scatter.6.cloned.1.call-update) | async-done | bytes 114704 | tf_op jit(solution)/shard_map/reduce_scatter | solution.py:91
  468.7 1.7 pad_maximum_fusion.17
  470.4 6.7 %all-to-all-start.2 = ((bf16[8,16,896]{2,1,0:T(8,128)(2,1)}), bf16[8,16,896]{2,1,0:T(8,128)(2,1)S(1)}, u32[]{:S(2)}, u32[]{:S(2)}) async-start(bf16[8,16,896]{2,1,0:T(8,128)(2,1)} %pad_maximum_fusion.17), calls=%async_computation.3 | async-start | bytes 458752 | tf_op jit(solution)/shard_map/all_to_all | solution.py:281
  477.1 72.7 %reduce-scatter.8.cloned.1.call-done = bf16[2,32,2304]{2,1,0:T(8,128)(2,1)} async-done(((bf16[2,512,2304]{2,1,0:T(8,128)(2,1)}), bf16[2,32,2304]{2,1,0:T(8,128)(2,1)}) %reduce-scatter.8.cloned.1.call-update) | async-done | bytes 294928 | tf_op jit(solution)/shard_map/reduce_scatter | solution.py:91
  549.8 1.9 pad_maximum_fusion.13
  551.8 7.0 %all-to-all-start.3 = ((bf16[8,16,2304]{2,1,0:T(8,128)(2,1)}), bf16[8,16,2304]{2,1,0:T(8,128)(2,1)S(1)}, u32[]{:S(2)}, u32[]{:S(2)}) async-start(bf16[8,16,2304]{2,1,0:T(8,128)(2,1)} %pad_maximum_fusion.13), calls=%async_computation.5 | async-start | bytes 1179648 | tf_op jit(solution)/shard_map/all_to_all | solution.py:281
  560.1 2.4 copy.76
  562.5 4.5 reshape.249
  569.9 1.4 reshape.253
  572.2 1.4 reshape.255
  (273 shorter events, 55.7 us)
Async XLA Ops:
  7.2 2.4 copy-start.59
  7.2 2.4 copy-start.58
  7.2 11.5 %copy-start.8 = (bf16[256,1024]{1,0:T(8,128)(2,1)S(1)}, bf16[256,1024]{1,0:T(8,128)(2,1)}, u32[]{:S(2)}) copy-start(bf16[256,1024]{1,0:T(8,128)(2,1)} %param.10) | copy-start | bytes 1572868
  7.2 57.7 %all-gather.4.cloned.1.call-start = ((), (), s32[]{:S(2)}) async-start(), calls=%async_computation.7 | async-start | bytes 1949696 | tf_op jit(solution)/shard_map/all_gather | solution.py:87
  8.9 25.4 %copy-start.51 = (bf16[16,4608]{1,0:T(8,128)(2,1)S(1)}, bf16[16,4608]{1,0:T(8,128)(2,1)}, u32[]{:S(2)}) copy-start(bf16[16,4608]{1,0:T(8,128)(2,1)} %param.16) | copy-start | bytes 442372
  9.7 25.4 %copy-start.52 = (bf16[16,4608]{1,0:T(8,128)(2,1)S(1)}, bf16[16,4608]{1,0:T(8,128)(2,1)}, u32[]{:S(2)}) copy-start(bf16[16,4608]{1,0:T(8,128)(2,1)} %param.17) | copy-start | bytes 442372
  18.0 121.6 %all-gather.8.cloned.1.call-start = ((), (), s32[]{:S(2)}) async-start(), calls=%async_computation.9 | async-start | bytes 2506752 | tf_op jit(solution)/shard_map/all_gather | solution.py:87
  18.7 12.5 %collective-permute-start = (bf16[256,1024]{1,0:T(8,128)(2,1)S(1)}, bf16[256,1024]{1,0:T(8,128)(2,1)S(1)}, u32[]{:S(2)}, u32[]{:S(2)}) collective-permute-start(bf16[256,1024]{1,0:T(8,128)(2,1)S(1)} %copy-done.8), channel_id=1, source_target_pairs={{0,32},{1,33},{2,34},{3,35},{4,36},{5,37},{6,38},{7,39},{8,40},{9,... | collective-permute-start | bytes 1572872 | tf_op jit(solution)/shard_map/ppermute | solution.py:44
  31.2 35.9 %copy-start.11 = (bf16[256,1024]{1,0:T(8,128)(2,1)}, bf16[256,1024]{1,0:T(8,128)(2,1)S(1)}, u32[]{:S(2)}) copy-start(bf16[256,1024]{1,0:T(8,128)(2,1)S(1)} %collective-permute-done) | copy-start | bytes 1572868
  32.4 7.9 %copy-start.55 = (bf16[16,3]{0,1:T(4,128)(2,1)S(1)}, bf16[16,3]{0,1:T(4,128)(2,1)}, u32[]{:S(2)}) copy-start(bf16[16,3]{0,1:T(4,128)(2,1)} %param.13) | copy-start | bytes 292
  32.4 8.0 %copy-start.54 = (bf16[16,1024]{1,0:T(8,128)(2,1)S(1)}, bf16[16,1024]{1,0:T(8,128)(2,1)}, u32[]{:S(2)}) copy-start(bf16[16,1024]{1,0:T(8,128)(2,1)} %param.14) | copy-start | bytes 98308
  32.4 30.1 %collective-permute-start.1 = (bf16[2,256,1024]{2,1,0:T(8,128)(2,1)}, bf16[2,256,1024]{2,1,0:T(8,128)(2,1)}, u32[]{:S(2)}, u32[]{:S(2)}) collective-permute-start(bf16[2,256,1024]{2,1,0:T(8,128)(2,1)} %pad_maximum_fusion.7), channel_id=1, source_target_pairs={{0,1},{1,0},{2,3},{3,2},{4,5},{5,4},{6,7},{7,6},{8,9},{9,8},{10,11... | collective-permute-start | bytes 3145736 | tf_op jit(solution)/shard_map/ppermute | solution.py:40
  36.8 24.8 %all-to-all-start.1 = ((bf16[4,16,2304]{2,1,0:T(8,128)(2,1)}), bf16[4,16,2304]{2,1,0:T(8,128)(2,1)S(1)}, u32[]{:S(2)}, u32[]{:S(2)}) async-start(bf16[4,16,2304]{2,1,0:T(8,128)(2,1)} %pad_maximum_fusion.16), calls=%async_computation.1 | async-start | bytes 589824 | tf_op jit(solution)/shard_map/all_to_all | solution.py:83
  40.2 129.2 %all-gather.6.cloned.1.call-start = ((), (), s32[]{:S(2)}) async-start(), calls=%async_computation.8 | async-start | bytes 5013504 | tf_op jit(solution)/shard_map/all_gather | solution.py:87
  62.3 253.1 %all-reduce.12.cloned.1.call-start = ((), (), s32[]{:S(2)}) async-start(), calls=%async_computation.12 | async-start | bytes 1179648
  63.8 3.3 copy-start.14
  63.8 3.3 copy-start.17
  67.1 2.3 copy-start.49
  72.5 8.2 %copy-start.2 = (f32[1024,256]{1,0:T(8,128)}, f32[1024,256]{1,0:T(8,128)S(1)}, u32[]{:S(2)}) copy-start(f32[1024,256]{1,0:T(8,128)S(1)} %get-tuple-element.97) | copy-start | bytes 3145732
  72.5 8.2 %copy-start.6 = (f32[1024,256]{1,0:T(8,128)}, f32[1024,256]{1,0:T(8,128)S(1)}, u32[]{:S(2)}) copy-start(f32[1024,256]{1,0:T(8,128)S(1)} %get-tuple-element.96) | copy-start | bytes 3145732
  73.7 5.8 %collective-permute-start.2 = (bf16[2,2,256]{2,1,0:T(2,128)(2,1)S(1)}, bf16[2,2,256]{2,1,0:T(2,128)(2,1)S(1)}, u32[]{:S(2)}, u32[]{:S(2)}) collective-permute-start(bf16[2,2,256]{2,1,0:T(2,128)(2,1)S(1)} %broadcast_select_fusion.7), channel_id=1, source_target_pairs={{0,2},{1,3},{2,4},{3,5},{4,6},{5,7},{6,8},{7,9},{8,10},{9,11},{10,... | collective-permute-start | bytes 6152 | tf_op jit(solution)/shard_map/ppermute | solution.py:180
  80.7 2.6 copy-start.34
  84.2 5.3 copy-start.22
  84.3 20.3 %collective-permute-start.3 = (bf16[2,256,1024]{2,1,0:T(8,128)(2,1)S(1)}, bf16[2,256,1024]{2,1,0:T(8,128)(2,1)S(1)}, u32[]{:S(2)}, u32[]{:S(2)}) collective-permute-start(bf16[2,256,1024]{2,1,0:T(8,128)(2,1)S(1)} %pad_maximum_fusion.8), channel_id=1, source_target_pairs={{0,1},{1,0},{2,3},{3,2},{4,5},{5,4},{6,7},{7,6},{8,9},{9,8},{10,11... | collective-permute-start | bytes 3145736 | tf_op jit(solution)/shard_map/ppermute | solution.py:40
  89.5 12.8 %collective-permute-start.8 = (bf16[256,1024]{1,0:T(8,128)(2,1)S(1)}, bf16[256,1024]{1,0:T(8,128)(2,1)S(1)}, u32[]{:S(2)}, u32[]{:S(2)}) collective-permute-start(bf16[256,1024]{1,0:T(8,128)(2,1)S(1)} %copy-done.22), channel_id=1, source_target_pairs={{0,32},{1,33},{2,34},{3,35},{4,36},{5,37},{6,38},{7,39},{8,40},{9,... | collective-permute-start | bytes 1572872 | tf_op jit(solution)/shard_map/ppermute | solution.py:44
  102.3 6.2 %collective-permute-start.9 = (bf16[2,256,1024]{2,1,0:T(8,128)(2,1)S(1)}, bf16[2,256,1024]{2,1,0:T(8,128)(2,1)S(1)}, u32[]{:S(2)}, u32[]{:S(2)}) collective-permute-start(bf16[2,256,1024]{2,1,0:T(8,128)(2,1)S(1)} %pad_maximum_fusion.10), channel_id=1, source_target_pairs={{0,1},{1,0},{2,3},{3,2},{4,5},{5,4},{6,7},{7,6},{8,9},{9,8},{10,11... | collective-permute-start | bytes 3145736 | tf_op jit(solution)/shard_map/ppermute | solution.py:40
  104.6 3.5 copy-start.9
  104.6 3.5 copy-start.12
  104.6 3.5 copy-start.15
  104.7 3.5 copy-start.18
  106.7 24.9 %collective-permute-start.4 = (bf16[2,256,1024]{2,1,0:T(8,128)(2,1)}, bf16[2,256,1024]{2,1,0:T(8,128)(2,1)}, u32[]{:S(2)}, u32[]{:S(2)}) collective-permute-start(bf16[2,256,1024]{2,1,0:T(8,128)(2,1)} %fusion.26), channel_id=1, source_target_pairs={{0,32},{1,33},{2,34},{3,35},{4,36},{5,37},{6,38},{7,39},{8,40},{9,... | collective-permute-start | bytes 3145736 | tf_op jit(solution)/shard_map/ppermute | solution.py:44
  108.5 2.9 copy-start
  111.6 21.6 %copy-start.30 = (f32[1,256,1024]{2,1,0:T(8,128)S(1)}, f32[1,256,1024]{2,1,0:T(8,128)}, u32[]{:S(2)}) copy-start(f32[1,256,1024]{2,1,0:T(8,128)} %get-tuple-element.92) | copy-start | bytes 3145732
  111.6 21.6 %copy-start.31 = (f32[1,256,1024]{2,1,0:T(8,128)S(1)}, f32[1,256,1024]{2,1,0:T(8,128)}, u32[]{:S(2)}) copy-start(f32[1,256,1024]{2,1,0:T(8,128)} %get-tuple-element.93) | copy-start | bytes 3145732
  137.0 11.4 %collective-permute-start.5 = (bf16[2,256,1024]{2,1,0:T(8,128)(2,1)}, bf16[2,256,1024]{2,1,0:T(8,128)(2,1)}, u32[]{:S(2)}, u32[]{:S(2)}) collective-permute-start(bf16[2,256,1024]{2,1,0:T(8,128)(2,1)} %multiply_convert_fusion.5), channel_id=1, source_target_pairs={{0,1},{1,0},{2,3},{3,2},{4,5},{5,4},{6,7},{7,6},{8,9},{9,8},{10,11... | collective-permute-start | bytes 3145736 | tf_op jit(solution)/shard_map/ppermute | solution.py:40
  169.4 5.3 copy-start.40
  169.4 5.3 copy-start.56
  181.2 2.9 copy-start.64
  181.2 2.9 copy-start.61
  181.2 38.7 %copy-start.63 = (bf16[1024,1152]{1,0:T(8,128)(2,1)}, bf16[1024,1152]{1,0:T(8,128)(2,1)S(1)}, u32[]{:S(2)}) copy-start(bf16[1024,1152]{1,0:T(8,128)(2,1)S(1)} %get-tuple-element.83) | copy-start | bytes 7077892
  187.2 3.0 collective-permute-start.10
  190.6 24.6 %collective-permute-start.11 = (bf16[2,256,1024]{2,1,0:T(8,128)(2,1)S(1)}, bf16[2,256,1024]{2,1,0:T(8,128)(2,1)S(1)}, u32[]{:S(2)}, u32[]{:S(2)}) collective-permute-start(bf16[2,256,1024]{2,1,0:T(8,128)(2,1)S(1)} %fusion.25), channel_id=1, source_target_pairs={{0,32},{1,33},{2,34},{3,35},{4,36},{5,37},{6,38},{7,39},{8,40},{9,... | collective-permute-start | bytes 3145736 | tf_op jit(solution)/shard_map/ppermute | solution.py:44
  216.1 2.6 copy-start.1
  216.7 3.2 copy-start.57
  218.7 6.9 %collective-permute-start.12 = (bf16[2,256,1024]{2,1,0:T(8,128)(2,1)S(1)}, bf16[2,256,1024]{2,1,0:T(8,128)(2,1)S(1)}, u32[]{:S(2)}, u32[]{:S(2)}) collective-permute-start(bf16[2,256,1024]{2,1,0:T(8,128)(2,1)S(1)} %get-tuple-element.71), channel_id=1, source_target_pairs={{0,1},{1,0},{2,3},{3,2},{4,5},{5,4},{6,7},{7,6},{8,9},{9,8},{10,11... | collective-permute-start | bytes 3145736 | tf_op jit(solution)/shard_map/ppermute | solution.py:40
  225.5 15.4 %collective-permute-start.6 = (bf16[2,256,1024]{2,1,0:T(8,128)(2,1)}, bf16[2,256,1024]{2,1,0:T(8,128)(2,1)}, u32[]{:S(2)}, u32[]{:S(2)}) collective-permute-start(bf16[2,256,1024]{2,1,0:T(8,128)(2,1)} %pad_maximum_fusion.9), channel_id=1, source_target_pairs={{0,1},{1,0},{2,3},{3,2},{4,5},{5,4},{6,7},{7,6},{8,9},{9,8},{10,11... | collective-permute-start | bytes 3145736 | tf_op jit(solution)/shard_map/ppermute | solution.py:40
  232.5 159.9 %reduce-scatter.10.cloned.1.call-start = ((), (), s32[]{:S(2)}) async-start(), calls=%async_computation.13 | async-start | bytes 2506752
  239.1 229.7 %reduce-scatter.6.cloned.1.call-start = ((), (), s32[]{:S(2)}) async-start(), calls=%async_computation.10 | async-start | bytes 1949696 | tf_op jit(solution)/shard_map/reduce_scatter | solution.py:91
  240.9 5.3 copy-start.28
  245.0 13.9 %collective-permute-start.7 = (bf16[256,1024]{1,0:T(8,128)(2,1)}, bf16[256,1024]{1,0:T(8,128)(2,1)}, u32[]{:S(2)}, u32[]{:S(2)}) collective-permute-start(bf16[256,1024]{1,0:T(8,128)(2,1)} %fusion.44), channel_id=1, source_target_pairs={{0,32},{1,33},{2,34},{3,35},{4,36},{5,37},{6,38},{7,39},{8,40},{9,... | collective-permute-start | bytes 1572872 | tf_op jit(solution)/shard_map/ppermute | solution.py:44
  246.2 15.4 %collective-permute-start.13 = (f32[2,2,256]{2,1,0:T(2,128)S(1)}, f32[2,2,256]{2,1,0:T(2,128)S(1)}, u32[]{:S(2)}, u32[]{:S(2)}) collective-permute-start(f32[2,2,256]{2,1,0:T(2,128)S(1)} %broadcast_select_fusion.4), channel_id=1, source_target_pairs={{0,30},{1,31},{2,0},{3,1},{4,2},{5,3},{6,4},{7,5},{8,6},{9,7},{10,... | collective-permute-start | bytes 12296 | tf_op jit(solution)/shard_map/ppermute | solution.py:235
  266.2 5.0 copy-start.43
  274.3 2.3 copy-start.41
  275.7 274.1 %reduce-scatter.8.cloned.1.call-start = ((), (), s32[]{:S(2)}) async-start(), calls=%async_computation.11 | async-start | bytes 5013504 | tf_op jit(solution)/shard_map/reduce_scatter | solution.py:91
  276.6 5.0 copy-start.62
  287.3 2.2 copy-start.60
  288.7 3.7 collective-permute-start.14
  292.9 102.4 %collective-permute-start.15 = (bf16[256,1024]{1,0:T(8,128)(2,1)S(1)}, bf16[256,1024]{1,0:T(8,128)(2,1)S(1)}, u32[]{:S(2)}, u32[]{:S(2)}) collective-permute-start(bf16[256,1024]{1,0:T(8,128)(2,1)S(1)} %fusion.45), channel_id=1, source_target_pairs={{0,32},{1,33},{2,34},{3,35},{4,36},{5,37},{6,38},{7,39},{8,40},{9,... | collective-permute-start | bytes 1572872 | tf_op jit(solution)/shard_map/ppermute | solution.py:44
  316.2 4.3 collective-permute-start.16
  392.5 4.4 copy-start.21
  392.5 166.3 %collective-permute-start.17 = (bf16[72,1024]{1,0:T(8,128)(2,1)}, bf16[72,1024]{1,0:T(8,128)(2,1)S(1)}, u32[]{:S(2)}, u32[]{:S(2)}) collective-permute-start(bf16[72,1024]{1,0:T(8,128)(2,1)} %reduce-scatter.10.cloned.1.call-done), channel_id=1, source_target_pairs={{0,64},{64,0},{1,65},{65,1},{2,66},{66,2},{3,67},{67,3},{4,68},{68... | collective-permute-start | bytes 442376 | tf_op jit(solution)/shard_map/ppermute | solution.py:292
  399.4 159.4 %copy-start.53 = (bf16[72,1024]{1,0:T(8,128)(2,1)S(1)}, bf16[72,1024]{1,0:T(8,128)(2,1)}, u32[]{:S(2)}) copy-start(bf16[72,1024]{1,0:T(8,128)(2,1)} %reduce-scatter.10.cloned.1.call-done) | copy-start | bytes 442372
  470.4 81.4 %all-to-all-start.2 = ((bf16[8,16,896]{2,1,0:T(8,128)(2,1)}), bf16[8,16,896]{2,1,0:T(8,128)(2,1)S(1)}, u32[]{:S(2)}, u32[]{:S(2)}) async-start(bf16[8,16,896]{2,1,0:T(8,128)(2,1)} %pad_maximum_fusion.17), calls=%async_computation.3 | async-start | bytes 458752 | tf_op jit(solution)/shard_map/all_to_all | solution.py:281
  551.8 17.2 %all-to-all-start.3 = ((bf16[8,16,2304]{2,1,0:T(8,128)(2,1)}), bf16[8,16,2304]{2,1,0:T(8,128)(2,1)S(1)}, u32[]{:S(2)}, u32[]{:S(2)}) async-start(bf16[8,16,2304]{2,1,0:T(8,128)(2,1)} %pad_maximum_fusion.13), calls=%async_computation.5 | async-start | bytes 1179648 | tf_op jit(solution)/shard_map/all_to_all | solution.py:281
  (29 other events, 44.5 us)
Sparse Core Ops, SparseCore 0:
  18.1 46.8 all-gather.3
  67.1 45.2 all-gather.7
  115.2 54.1 all-gather.5
  232.7 82.7 all-reduce.11
  318.6 73.8 reduce-scatter.9
  395.5 73.1 reduce-scatter.5
  472.1 77.7 reduce-scatter.7
